TPU v7x, 32 devices: a whole 2x2x4 slice. The times are simulated.
32 devices in a mesh: gx: 8 (over z, core), gy: 4 (over y, x).
Axes of the slice: x: 2, y: 2, z: 4, core: 2. Of those that a mesh axis runs over, the one named last changes fastest.
Arguments:
- obj_field: float32 [2, 2, 2048, 4096], P(None, None, 'gy', 'gx'), may hold values from -0.8 to 0.8
- probe_modes: float32 [2, 2, 256, 256], P(None, None, 'gx'), may hold values from -6 to 6
- positions: int32 [4, 8, 6, 2], P('gy', 'gx'), may hold values from 0 to 511
- counts: int32 [4, 8], P('gy', 'gx'), may hold values from 1 to 6, as said below
- amplitudes: float32 [4, 8, 6, 256, 256], P('gy', 'gx'), may hold values from 0.6 to 1.8
Outputs:
- obj_grad: float32 [2, 2, 2048, 4096], P(None, None, 'gy', 'gx')
- probe_grad: float32 [2, 2, 256, 256], P(None, None, 'gx')
Inputs may be any that keep to these rules, and one draw needn't show every extreme that they name: `counts`: each tile has between 1 and 6 used slots and at least one tile uses all 6.
All inputs are finite; a program needn't handle non-finite values.
Results may differ from a plain program's by a relative error of at most 0.00014.
Values sent between devices are 32-bit elements; how exact they have to be, the bound alone decides.
A program may use at most 128 MiB of HBM per device.

v0:
```python
import math

import jax
import jax.numpy as jnp
from jax import lax
from jax.sharding import PartitionSpec as P

BAND = 48


def shifted(x, axis, by):
    length = lax.axis_size(axis)
    pairs = [(i, i + by) for i in range(length) if 0 <= i + by < length]
    return lax.ppermute(x, axis, pairs)


def tables_for(probe_len):
    indices = jnp.arange(probe_len, dtype=jnp.int32)
    offsets = (indices[:, None] - indices[None, :]).astype(jnp.float32)
    chirp = math.pi * offsets * offsets / (2.0 * BAND)
    inside = jnp.where(jnp.abs(offsets) <= BAND, 1.0, 0.0).astype(jnp.float32) / math.sqrt(
        2.0 * BAND + 1.0
    )
    cycles = (indices[:, None] * indices[None, :] % probe_len).astype(jnp.float32)
    angles = -2.0 * math.pi * cycles / probe_len
    scaling = 1.0 / math.sqrt(probe_len)
    return (
        jnp.cos(chirp) * inside,
        jnp.sin(chirp) * inside,
        jnp.cos(angles) * scaling,
        jnp.sin(angles) * scaling,
    )


def left_apply(mat_re, mat_im, wave_re, wave_im):
    highest = lax.Precision.HIGHEST
    out_re = jnp.einsum("ab,mbc->mac", mat_re, wave_re, precision=highest) - jnp.einsum(
        "ab,mbc->mac", mat_im, wave_im, precision=highest
    )
    out_im = jnp.einsum("ab,mbc->mac", mat_re, wave_im, precision=highest) + jnp.einsum(
        "ab,mbc->mac", mat_im, wave_re, precision=highest
    )
    return (out_re, out_im)


def right_apply(mat_re, mat_im, wave_re, wave_im):
    highest = lax.Precision.HIGHEST
    out_re = jnp.einsum("mab,bc->mac", wave_re, mat_re, precision=highest) - jnp.einsum(
        "mab,bc->mac", wave_im, mat_im, precision=highest
    )
    out_im = jnp.einsum("mab,bc->mac", wave_im, mat_re, precision=highest) + jnp.einsum(
        "mab,bc->mac", wave_re, mat_im, precision=highest
    )
    return (out_re, out_im)


def position_loss(window, mode_set, amplitude, weight, tables):
    prop_re, prop_im, four_re, four_im = tables
    wave_re = mode_set[:, 0] * window[0, 0] - mode_set[:, 1] * window[0, 1]
    wave_im = mode_set[:, 0] * window[0, 1] + mode_set[:, 1] * window[0, 0]
    wave_re, wave_im = left_apply(prop_re, prop_im, wave_re, wave_im)
    wave_re, wave_im = right_apply(prop_re, prop_im, wave_re, wave_im)
    trans_re = window[1, 0]
    trans_im = window[1, 1]
    wave_re, wave_im = (
        wave_re * trans_re - wave_im * trans_im,
        wave_re * trans_im + wave_im * trans_re,
    )
    far_re, far_im = left_apply(four_re, four_im, wave_re, wave_im)
    far_re, far_im = right_apply(four_re, four_im, far_re, far_im)
    intensity = jnp.sum(far_re * far_re + far_im * far_im, axis=0)
    misfit = jnp.sqrt(intensity + 1.0) - amplitude
    return weight * jnp.sum(misfit * misfit)


def on_device(obj_field, probe_modes, positions, counts, amplitudes):
    probe_full = lax.all_gather(probe_modes, "gx", axis=2, tiled=True)
    probe_len = probe_full.shape[3]
    tile_len = obj_field.shape[2]
    layers = obj_field.shape[0]
    slot_total = amplitudes.shape[2]
    tables = tables_for(probe_len)
    right_part = shifted(obj_field[:, :, :, :probe_len], "gx", -1)
    lower_part = shifted(obj_field[:, :, :probe_len, :], "gy", -1)
    corner_step = shifted(obj_field[:, :, :probe_len, :probe_len], "gx", -1)
    corner_part = shifted(corner_step, "gy", -1)
    upper_half = jnp.concatenate([obj_field, right_part], axis=3)
    lower_half = jnp.concatenate([lower_part, corner_part], axis=3)
    extended = jnp.concatenate([upper_half, lower_half], axis=2)
    active = counts[0, 0]
    anchor = jnp.int32(0)
    block_shape = (layers, 2, probe_len, probe_len)

    def starts_of(number):
        return (anchor, anchor, positions[0, 0, number, 0], positions[0, 0, number, 1])

    def visit(number, running, weight):
        grad_ext, grad_probe = running
        starts = starts_of(number)
        window = lax.dynamic_slice(extended, starts, block_shape)
        window_grad, modes_grad = jax.grad(position_loss, argnums=(0, 1))(
            window, probe_full, amplitudes[0, 0, number], weight, tables
        )
        current = lax.dynamic_slice(grad_ext, starts, block_shape)
        grad_ext = lax.dynamic_update_slice(grad_ext, current + window_grad, starts)
        return (grad_ext, grad_probe + modes_grad)

    initial = (jnp.zeros_like(extended), jnp.zeros_like(probe_full))

    def masked_visit(number, running):
        weight = jnp.where(number < active, 1.0, 0.0).astype(jnp.float32)
        return visit(number, running, weight)

    grad_ext, grad_probe = lax.fori_loop(0, slot_total, masked_visit, initial)
    back_right = shifted(grad_ext[:, :, :tile_len, tile_len:], "gx", 1)
    back_lower = shifted(grad_ext[:, :, tile_len:, :tile_len], "gy", 1)
    corner_back = shifted(grad_ext[:, :, tile_len:, tile_len:], "gx", 1)
    back_corner = shifted(corner_back, "gy", 1)
    obj_grad = grad_ext[:, :, :tile_len, :tile_len]
    obj_grad = obj_grad.at[:, :, :, :probe_len].add(back_right)
    obj_grad = obj_grad.at[:, :, :probe_len, :].add(back_lower)
    obj_grad = obj_grad.at[:, :, :probe_len, :probe_len].add(back_corner)
    column_sum = lax.psum(grad_probe, "gy")
    probe_grad = lax.psum_scatter(column_sum, "gx", scatter_dimension=2, tiled=True)
    return (obj_grad, probe_grad)


def solution(mesh):
    return jax.shard_map(
        on_device,
        mesh=mesh,
        in_specs=(
            P(None, None, "gy", "gx"),
            P(None, None, "gx", None),
            P("gy", "gx", None, None),
            P("gy", "gx"),
            P("gy", "gx", None, None, None),
        ),
        out_specs=(P(None, None, "gy", "gx"), P(None, None, "gx", None)),
        check_vma=False,
    )
```

profile of v0, /device:TPU:20, one launch (start us, length us, event | category | flops | bytes accessed | tf_op | source)
XLA Modules:
  0.0 740.3 jit_solution(10115234302217868427)
XLA Ops:
  10.8 3.1 slice.161
  13.9 3.3 collective-permute-start.1
  23.1 3.3 collective-permute-start.3
  26.4 21.3 %all-gather.2.cloned.1.call-done = f32[2,2,256,256]{3,1,0,2:T(2,128)} async-done(((f32[2,2,32,256]{3,1,0,2:T(2,128)}), f32[2,2,256,256]{3,1,0,2:T(2,128)}) %all-gather.2.cloned.1.call-update) | async-done | bytes 1048592 | tf_op jit(solution)/shard_map/all_gather | solution.py:77
  49.2 37.4 %collective-permute-done.3 = f32[2,2,256,256]{3,2,1,0:T(8,128)} collective-permute-done((f32[2,2,256,256]{3,2,1,0:T(8,128)}, f32[2,2,256,256]{3,2,1,0:T(8,128)}, u32[]{:S(2)}, u32[]{:S(2)}) %collective-permute-start.3) | collective-permute-done | bytes 1048608 | tf_op jit(solution)/shard_map/ppermute | solution.py:14
  86.6 6.1 maximum_maximum_fusion
  92.7 4.5 broadcast_in_dim.94
  97.2 529.0 %while.20 = (s32[]{:T(128)}, f32[2,2,768,768]{3,2,1,0:T(8,128)}, f32[2,2,256,256]{2,3,0,1:T(8,128)}, s32[1,1,6,2]{2,3,1,0:T(2,128)S(1)}, f32[2,2,256,256]{2,3,0,...) while((s32[]{:T(128)}, f32[2,2,768,768]{3,2,1,0:T(8,128)}, ...), condition=%wide.region_10.11_spmd.clone.clone, body=%wide.region_0.10_spmd.clone.clone.sunk | while | flops 12925992960 | bytes 81264944 | solution.py:114
  160.7 3.8 multiply_bitcast_fusion.5
  172.7 11.9 %dynamic_update_slice.10 = f32[2,2,768,768]{3,2,1,0:T(8,128)} dynamic-update-slice(f32[2,2,768,768]{3,2,1,0:T(8,128)} %get-tuple-element.593, f32[2,2,256,256]{3,2,1,0:T(8,128)S(1)} %add_add_fusion.2, s32[]{:T(128)} %constant.155.clone.1..sunk, s32[]{:T(128)} %constant.155.clone.1..sunk, s32[]{:T(128)S(6)} %select_n.311, s32[]{:T(128)S(6)} %select_n.312) | dynamic-update-slice | bytes 2097156 | tf_op jit(solution)/shard_map/while/body/eval_jaxpr/dynamic_update_slice | solution.py:105
  248.1 3.8 multiply_bitcast_fusion.5
  257.6 2.7 select_add_fusion.2
  260.4 11.2 %dynamic_update_slice.10 = f32[2,2,768,768]{3,2,1,0:T(8,128)} dynamic-update-slice(f32[2,2,768,768]{3,2,1,0:T(8,128)} %get-tuple-element.593, f32[2,2,256,256]{3,2,1,0:T(8,128)S(1)} %add_add_fusion.2, s32[]{:T(128)} %constant.155.clone.1..sunk, s32[]{:T(128)} %constant.155.clone.1..sunk, s32[]{:T(128)S(6)} %select_n.311, s32[]{:T(128)S(6)} %select_n.312) | dynamic-update-slice | bytes 2097156 | tf_op jit(solution)/shard_map/while/body/eval_jaxpr/dynamic_update_slice | solution.py:105
  335.3 3.8 multiply_bitcast_fusion.5
  347.5 12.0 %dynamic_update_slice.10 = f32[2,2,768,768]{3,2,1,0:T(8,128)} dynamic-update-slice(f32[2,2,768,768]{3,2,1,0:T(8,128)} %get-tuple-element.593, f32[2,2,256,256]{3,2,1,0:T(8,128)S(1)} %add_add_fusion.2, s32[]{:T(128)} %constant.155.clone.1..sunk, s32[]{:T(128)} %constant.155.clone.1..sunk, s32[]{:T(128)S(6)} %select_n.311, s32[]{:T(128)S(6)} %select_n.312) | dynamic-update-slice | bytes 2097156 | tf_op jit(solution)/shard_map/while/body/eval_jaxpr/dynamic_update_slice | solution.py:105
  423.3 3.8 multiply_bitcast_fusion.5
  432.9 2.7 select_add_fusion.2
  435.6 12.3 %dynamic_update_slice.10 = f32[2,2,768,768]{3,2,1,0:T(8,128)} dynamic-update-slice(f32[2,2,768,768]{3,2,1,0:T(8,128)} %get-tuple-element.593, f32[2,2,256,256]{3,2,1,0:T(8,128)S(1)} %add_add_fusion.2, s32[]{:T(128)} %constant.155.clone.1..sunk, s32[]{:T(128)} %constant.155.clone.1..sunk, s32[]{:T(128)S(6)} %select_n.311, s32[]{:T(128)S(6)} %select_n.312) | dynamic-update-slice | bytes 2097156 | tf_op jit(solution)/shard_map/while/body/eval_jaxpr/dynamic_update_slice | solution.py:105
  511.4 3.8 multiply_bitcast_fusion.5
  523.7 12.0 %dynamic_update_slice.10 = f32[2,2,768,768]{3,2,1,0:T(8,128)} dynamic-update-slice(f32[2,2,768,768]{3,2,1,0:T(8,128)} %get-tuple-element.593, f32[2,2,256,256]{3,2,1,0:T(8,128)S(1)} %add_add_fusion.2, s32[]{:T(128)} %constant.155.clone.1..sunk, s32[]{:T(128)} %constant.155.clone.1..sunk, s32[]{:T(128)S(6)} %select_n.311, s32[]{:T(128)S(6)} %select_n.312) | dynamic-update-slice | bytes 2097156 | tf_op jit(solution)/shard_map/while/body/eval_jaxpr/dynamic_update_slice | solution.py:105
  599.4 3.8 multiply_bitcast_fusion.5
  611.6 11.7 %dynamic_update_slice.10 = f32[2,2,768,768]{3,2,1,0:T(8,128)} dynamic-update-slice(f32[2,2,768,768]{3,2,1,0:T(8,128)} %get-tuple-element.593, f32[2,2,256,256]{3,2,1,0:T(8,128)S(1)} %add_add_fusion.2, s32[]{:T(128)} %constant.155.clone.1..sunk, s32[]{:T(128)} %constant.155.clone.1..sunk, s32[]{:T(128)S(6)} %select_n.311, s32[]{:T(128)S(6)} %select_n.312) | dynamic-update-slice | bytes 2097156 | tf_op jit(solution)/shard_map/while/body/eval_jaxpr/dynamic_update_slice | solution.py:105
  628.8 3.1 slice.165
  631.9 2.9 collective-permute-start.4
  634.8 3.1 slice.167
  641.2 3.7 collective-permute-start.6
  644.9 35.7 %collective-permute-done.6 = f32[2,2,256,256]{3,2,1,0:T(8,128)} collective-permute-done((f32[2,2,256,256]{3,2,1,0:T(8,128)S(1)}, f32[2,2,256,256]{3,2,1,0:T(8,128)}, u32[]{:S(2)}, u32[]{:S(2)}) %collective-permute-start.6) | collective-permute-done | bytes 1048608 | tf_op jit(solution)/shard_map/ppermute | solution.py:14
  682.5 4.7 slice.163
  687.2 3.2 add_dynamic-update-slice_fusion
  690.4 4.3 constant_dynamic-update-slice_fusion
  694.7 17.0 %collective-permute-done.7 = f32[2,2,256,256]{3,2,1,0:T(8,128)S(1)} collective-permute-done((f32[2,2,256,256]{3,2,1,0:T(8,128)}, f32[2,2,256,256]{3,2,1,0:T(8,128)S(1)}, u32[]{:S(2)}, u32[]{:S(2)}) %collective-permute-start.7) | collective-permute-done | bytes 1048608 | tf_op jit(solution)/shard_map/ppermute | solution.py:14
  712.8 19.1 %all-reduce.12.cloned.1.call-done = f32[2,2,32,256]{3,2,1,0:T(8,128)} async-done(((f32[2,2,32,256]{3,2,1,0:T(8,128)}), f32[2,2,32,256]{3,2,1,0:T(8,128)}) %all-reduce.12.cloned.1.call-update) | async-done | bytes 131088 | tf_op jit(solution)/shard_map/psum | solution.py:123
  (287 shorter events, 418.1 us)
Async XLA Ops:
  7.2 40.6 %all-gather.2.cloned.1.call-start = ((), (), s32[]{:S(2)}) async-start(), calls=%async_computation.1 | async-start | bytes 1179648 | tf_op jit(solution)/shard_map/all_gather | solution.py:77
  7.2 10.0 %copy-start = (f32[2,2,512,512]{3,2,1,0:T(8,128)S(1)}, f32[2,2,512,512]{3,2,1,0:T(8,128)}, u32[]{:S(2)}) copy-start(f32[2,2,512,512]{3,2,1,0:T(8,128)} %param.13) | copy-start | bytes 12582916
  8.7 12.3 %copy-start.1 = (f32[2,2,32,256]{3,2,1,0:T(8,128)S(1)}, f32[2,2,32,256]{3,2,1,0:T(8,128)}, u32[]{:S(2)}) copy-start(f32[2,2,32,256]{3,2,1,0:T(8,128)} %param.14) | copy-start | bytes 393220
  8.7 14.4 %collective-permute-start.2 = (f32[2,2,256,256]{3,2,1,0:T(8,128)S(1)}, f32[2,2,256,256]{3,2,1,0:T(8,128)}, u32[]{:S(2)}, u32[]{:S(2)}) collective-permute-start(f32[2,2,256,256]{3,2,1,0:T(8,128)S(1)} %slice.162), channel_id=1, source_target_pairs={{4,0},{8,4},{12,8},{16,12},{20,16},{24,20},{28,24},{5,1},{9,5},{13... | collective-permute-start | bytes 3145736 | tf_op jit(solution)/shard_map/ppermute | solution.py:14
  13.9 72.7 %collective-permute-start.1 = (f32[2,2,256,512]{3,2,1,0:T(8,128)}, f32[2,2,256,512]{3,2,1,0:T(8,128)S(1)}, u32[]{:S(2)}, u32[]{:S(2)}) collective-permute-start(f32[2,2,256,512]{3,2,1,0:T(8,128)} %slice.161), channel_id=1, source_target_pairs={{1,0},{2,1},{3,2},{5,4},{6,5},{7,6},{9,8},{10,9},{11,10},{13,12},{... | collective-permute-start | bytes 6291464 | tf_op jit(solution)/shard_map/ppermute | solution.py:14
  18.8 67.8 %collective-permute-start = (f32[2,2,512,256]{3,2,1,0:T(8,128)}, f32[2,2,512,256]{3,2,1,0:T(8,128)}, u32[]{:S(2)}, u32[]{:S(2)}) collective-permute-start(f32[2,2,512,256]{3,2,1,0:T(8,128)} %slice.160), channel_id=1, source_target_pairs={{4,0},{8,4},{12,8},{16,12},{20,16},{24,20},{28,24},{5,1},{9,5},{13... | collective-permute-start | bytes 6291464 | tf_op jit(solution)/shard_map/ppermute | solution.py:14
  21.8 665.4 %reduce-scatter.2.cloned.1.call-start = ((), (), s32[]{:S(2)}) async-start(), calls=%async_computation.2 | async-start | bytes 1179648 | tf_op jit(solution)/shard_map/reduce_scatter | solution.py:124
  23.1 63.5 %collective-permute-start.3 = (f32[2,2,256,256]{3,2,1,0:T(8,128)}, f32[2,2,256,256]{3,2,1,0:T(8,128)}, u32[]{:S(2)}, u32[]{:S(2)}) collective-permute-start(f32[2,2,256,256]{3,2,1,0:T(8,128)} %collective-permute-done.2), channel_id=1, source_target_pairs={{1,0},{2,1},{3,2},{5,4},{6,5},{7,6},{9,8},{10,9},{11,10},{13,12},{... | collective-permute-start | bytes 3145736 | tf_op jit(solution)/shard_map/ppermute | solution.py:14
  92.7 4.5 copy-start.2
  628.7 103.3 %all-reduce.12.cloned.1.call-start = ((), (), s32[]{:S(2)}) async-start(), calls=%async_computation.3 | async-start | bytes 262144 | tf_op jit(solution)/shard_map/psum | solution.py:123
  631.9 55.3 %collective-permute-start.4 = (f32[2,2,512,256]{3,2,1,0:T(8,128)}, f32[2,2,512,256]{3,2,1,0:T(8,128)S(1)}, u32[]{:S(2)}, u32[]{:S(2)}) collective-permute-start(f32[2,2,512,256]{3,2,1,0:T(8,128)} %slice.165), channel_id=1, source_target_pairs={{0,4},{4,8},{8,12},{12,16},{16,20},{20,24},{24,28},{1,5},{5,9},{9,... | collective-permute-start | bytes 6291464 | tf_op jit(solution)/shard_map/ppermute | solution.py:14
  637.9 52.5 %collective-permute-start.5 = (f32[2,2,256,512]{3,2,1,0:T(8,128)}, f32[2,2,256,512]{3,2,1,0:T(8,128)}, u32[]{:S(2)}, u32[]{:S(2)}) collective-permute-start(f32[2,2,256,512]{3,2,1,0:T(8,128)} %slice.167), channel_id=1, source_target_pairs={{0,1},{1,2},{2,3},{4,5},{5,6},{6,7},{8,9},{9,10},{10,11},{12,13},{... | collective-permute-start | bytes 6291464 | tf_op jit(solution)/shard_map/ppermute | solution.py:14
  641.2 39.4 %collective-permute-start.6 = (f32[2,2,256,256]{3,2,1,0:T(8,128)S(1)}, f32[2,2,256,256]{3,2,1,0:T(8,128)}, u32[]{:S(2)}, u32[]{:S(2)}) collective-permute-start(f32[2,2,256,256]{3,2,1,0:T(8,128)S(1)} %slice.169), channel_id=1, source_target_pairs={{0,4},{4,8},{8,12},{12,16},{16,20},{20,24},{24,28},{1,5},{5,9},{9,... | collective-permute-start | bytes 3145736 | tf_op jit(solution)/shard_map/ppermute | solution.py:14
  680.6 31.1 %collective-permute-start.7 = (f32[2,2,256,256]{3,2,1,0:T(8,128)}, f32[2,2,256,256]{3,2,1,0:T(8,128)S(1)}, u32[]{:S(2)}, u32[]{:S(2)}) collective-permute-start(f32[2,2,256,256]{3,2,1,0:T(8,128)} %collective-permute-done.6), channel_id=1, source_target_pairs={{0,1},{1,2},{2,3},{4,5},{5,6},{6,7},{8,9},{9,10},{10,11},{12,13},{... | collective-permute-start | bytes 3145736 | tf_op jit(solution)/shard_map/ppermute | solution.py:14
Sparse Core Ops, SparseCore 0:
  21.9 25.7 all-gather.1
  628.8 29.7 reduce-scatter.1
  687.3 44.6 all-reduce.11
where the time goes:
time: 749 us; the launch traced here: 740 us
  matrix products  347 us (46%)
  local copies, waits for them, and re-layouts  137 us (18%)
  waiting for transfers between devices  132 us (18%)
  other arithmetic  55.7 us (7%)
  loops' own time  33 us (4%)
  starting transfers between devices  21.4 us (3%)
  between operations  14.2 us (2%)
    ppermute x8, waiting for transfers between devices, shifted(): return lax.ppermute(x, axis, pairs)  91.3 us
    dynamic_update_slice x6, local copies, waits for them, and re-layouts, visit(): grad_ext = lax.dynamic_update_slice(grad_ext, current + window_grad, starts)  71.3 us
    dot_general x24, matrix products, left_apply(): jnp.einsum('ab,mbc->mac', mat_im, wave_im, precision=highest)  54.9 us
    dot_general x24, matrix products, right_apply(): jnp.einsum('mab,bc->mac', wave_im, mat_re, precision=highest)  43.6 us
    dot_general x24, matrix products, right_apply(): jnp.einsum('mab,bc->mac', wave_im, mat_im, precision=highest)  42.4 us
    dot_general x24, matrix products, left_apply(): jnp.einsum('ab,mbc->mac', mat_re, wave_re, precision=highest)  42 us
    dot_general x24, matrix products, left_apply(): jnp.einsum('ab,mbc->mac', mat_im, wave_re, precision=highest)  41.4 us
    dot_general x24, matrix products, left_apply(): jnp.einsum('ab,mbc->mac', mat_re, wave_im, precision=highest)  41.3 us
  transfers between devices with their start and end apart: 11, of which 6 were waited for; matrix products, arithmetic and copies ran while one was open for 4% of the time, Pallas kernels for 0%

commit v1 on v0

v1 whole, which is shorter than its diff:
```python
import functools
import math

import jax
import jax.numpy as jnp
import numpy as np
from jax import lax
from jax.experimental import pallas as pl
from jax.experimental.pallas import tpu as pltpu
from jax.sharding import PartitionSpec as P

BAND = 48
LANES = 128
ROWS = 8
VMEM_BYTES = 56 * 1024 * 1024


def shifted(x, axis, by):
    length = lax.axis_size(axis)
    pairs = [(i, i + by) for i in range(length) if 0 <= i + by < length]
    return lax.ppermute(x, axis, pairs)


def real_form(mat):
    full = np.block([[mat.real, -mat.imag], [mat.imag, mat.real]])
    parts = []
    for form in (full, full.T):
        form = form.astype(np.float32)
        high = form.astype(jnp.bfloat16)
        low = (form - high.astype(np.float32)).astype(jnp.bfloat16)
        parts += [high, low]
    return np.stack(parts)


def tables_for(probe_len):
    indices = np.arange(probe_len)
    offsets = (indices[:, None] - indices[None, :]).astype(np.float64)
    prop = np.where(
        np.abs(offsets) <= BAND, np.exp(1j * math.pi * offsets * offsets / (2.0 * BAND)), 0.0
    ) / math.sqrt(2.0 * BAND + 1.0)
    cycles = (indices[:, None] * indices[None, :]) % probe_len
    four = np.exp(-2j * math.pi * cycles / probe_len) / math.sqrt(probe_len)
    return real_form(prop), real_form(four)


def split(x):
    high = x.astype(jnp.bfloat16)
    low = (x - high.astype(jnp.float32)).astype(jnp.bfloat16)
    return high, low


def dot(a, b):
    return jnp.dot(a, b, preferred_element_type=jnp.float32)


def left(table, which, x):
    high, low = split(x)
    return dot(table[which], high) + dot(table[which], low) + dot(table[which + 1], high)


def right(x, table, which):
    high, low = split(x)
    return dot(high, table[which]) + dot(low, table[which]) + dot(high, table[which + 1])


def blocks(x):
    h = x.shape[0] // 2
    return x[:h, :h], x[:h, h:], x[h:, :h], x[h:, h:]


def joined(a, b, c, d):
    return jnp.concatenate(
        [jnp.concatenate([a, b], axis=1), jnp.concatenate([c, d], axis=1)], axis=0
    )


def swapped(x):
    a, b, c, d = blocks(x)
    return joined(a, c, b, d)


def window_of(ext, plane, row, col, size):
    base = pl.multiple_of(col // LANES * LANES, LANES)
    top = pl.multiple_of(row // ROWS * ROWS, ROWS)
    off, down = col - base, row - top
    wide = ext[plane, pl.ds(top, size + ROWS), pl.ds(base, size + LANES)]
    tall = wide.reshape(size // ROWS + 1, ROWS, size + LANES)
    tall = pltpu.roll(tall, lax.rem(ROWS - down, ROWS), 1)
    keep = lax.broadcasted_iota(jnp.int32, (1, ROWS, size + LANES), 1) < ROWS - down
    wide = jnp.where(keep, tall[:-1], tall[1:]).reshape(size, size + LANES)
    count = size // LANES
    turn = lax.rem(LANES - off, LANES)
    turned = [
        pltpu.roll(wide[:, k * LANES : (k + 1) * LANES], turn, 1) for k in range(count + 1)
    ]
    keep = lax.broadcasted_iota(jnp.int32, (size, LANES), 1) < LANES - off
    return jnp.concatenate(
        [jnp.where(keep, turned[k], turned[k + 1]) for k in range(count)], axis=1
    )


def add_window(ext, plane, row, col, grad):
    size = grad.shape[0]
    base = pl.multiple_of(col // LANES * LANES, LANES)
    top = pl.multiple_of(row // ROWS * ROWS, ROWS)
    off, down = col - base, row - top
    count = size // LANES
    turned = [pltpu.roll(grad[:, k * LANES : (k + 1) * LANES], off, 1) for k in range(count)]
    keep = lax.broadcasted_iota(jnp.int32, (size, LANES), 1) >= off
    zero = jnp.zeros((size, LANES), jnp.float32)
    turned = [zero] + turned + [zero]
    wide = jnp.concatenate(
        [jnp.where(keep, turned[k + 1], turned[k]) for k in range(count + 1)], axis=1
    )
    tall = pltpu.roll(wide.reshape(size // ROWS, ROWS, size + LANES), down, 1)
    keep = lax.broadcasted_iota(jnp.int32, (1, ROWS, size + LANES), 1) >= down
    zero = jnp.zeros((1, ROWS, size + LANES), jnp.float32)
    above = jnp.concatenate([zero, tall], axis=0)
    here = jnp.concatenate([tall, zero], axis=0)
    wide = jnp.where(keep, here, above).reshape(size + ROWS, size + LANES)
    ext[plane, pl.ds(top, size + ROWS), pl.ds(base, size + LANES)] += wide


def regions(ext, tile, size):
    return (
        ext.at[:, pl.ds(0, tile), pl.ds(0, tile)],
        ext.at[:, pl.ds(0, tile), pl.ds(tile, size)],
        ext.at[:, pl.ds(tile, size), pl.ds(0, tile)],
        ext.at[:, pl.ds(tile, size), pl.ds(tile, size)],
    )


def fetch(pieces, ext, sems, tile, size):
    copies = [
        pltpu.make_async_copy(piece, region, sems.at[k])
        for k, (piece, region) in enumerate(zip(pieces, regions(ext, tile, size)))
    ]
    for copy in copies:
        copy.start()
    for copy in copies:
        copy.wait()


def flush(ext, pieces, sems, tile, size):
    copies = [
        pltpu.make_async_copy(region, piece, sems.at[k])
        for k, (piece, region) in enumerate(zip(pieces, regions(ext, tile, size)))
    ]
    for copy in copies:
        copy.start()
    for copy in copies:
        copy.wait()


def forward_kernel(tile, size, cnt, pos, own, rgt, low, cor, probe, table, out, ext, sems):
    j = pl.program_id(0)

    @pl.when(j == 0)
    def _():
        fetch((own, rgt, low, cor), ext, sems, tile, size)

    @pl.when(j < cnt[0])
    def _():
        row, col = pos[2 * j], pos[2 * j + 1]
        wr = window_of(ext, 0, row, col, size)
        wi = window_of(ext, 1, row, col, size)
        waves = []
        for m in range(2):
            pr, pi = probe[m, 0], probe[m, 1]
            waves += [pr * wr - pi * wi, pr * wi + pi * wr]
        x = right(joined(*waves), table, 2)
        out[0] = left(table, 0, swapped(x))


def middle_kernel(
    tile, size, cnt, pos, own, rgt, low, cor, wave, amp, table,
    gwave, g_own, g_rgt, g_low, g_cor, ext, gext, sems,
):
    j = pl.program_id(0)

    @pl.when(j == 0)
    def _():
        fetch((own, rgt, low, cor), ext, sems, tile, size)
        gext[...] = jnp.zeros_like(gext)

    @pl.when(j < cnt[0])
    def _():
        row, col = pos[2 * j], pos[2 * j + 1]
        wr = window_of(ext, 0, row, col, size)
        wi = window_of(ext, 1, row, col, size)
        u0r, u1r, u0i, u1i = blocks(wave[0])
        x = joined(
            u0r * wr - u0i * wi, u1r * wr - u1i * wi, u0r * wi + u0i * wr, u1r * wi + u1i * wr
        )
        x = right(swapped(left(table, 0, x)), table, 2)
        p0r, p0i, p1r, p1i = blocks(x)
        intensity = p0r * p0r + p0i * p0i + p1r * p1r + p1i * p1i
        scale = 2.0 - 2.0 * amp[0] * lax.rsqrt(intensity + 1.0)
        g = joined(p0r * scale, p0i * scale, p1r * scale, p1i * scale)
        g = left(table, 2, swapped(right(g, table, 0)))
        g0r, g1r, g0i, g1i = blocks(g)
        u0r, u1r, u0i, u1i = blocks(wave[0])
        add_window(gext, 0, row, col, u0r * g0r + u0i * g0i + u1r * g1r + u1i * g1i)
        add_window(gext, 1, row, col, u0r * g0i - u0i * g0r + u1r * g1i - u1i * g1r)
        wr = window_of(ext, 0, row, col, size)
        wi = window_of(ext, 1, row, col, size)
        gwave[0] = joined(
            wr * g0r + wi * g0i, wr * g1r + wi * g1i, wr * g0i - wi * g0r, wr * g1i - wi * g1r
        )

    @pl.when(j == pl.num_programs(0) - 1)
    def _():
        flush(gext, (g_own, g_rgt, g_low, g_cor), sems, tile, size)


def backward_kernel(
    tile, size, cnt, pos, own, rgt, low, cor, gwave, probe, table,
    g_probe, g_own, g_rgt, g_low, g_cor, ext, gext, sems,
):
    j = pl.program_id(0)

    @pl.when(j == 0)
    def _():
        fetch((own, rgt, low, cor), ext, sems, tile, size)
        gext[...] = jnp.zeros_like(gext)
        g_probe[...] = jnp.zeros_like(g_probe)

    @pl.when(j < cnt[0])
    def _():
        row, col = pos[2 * j], pos[2 * j + 1]
        g = left(table, 2, gwave[0])
        g = right(swapped(g), table, 0)
        parts = blocks(g)
        wr = window_of(ext, 0, row, col, size)
        wi = window_of(ext, 1, row, col, size)
        sum_r, sum_i = 0.0, 0.0
        for m in range(2):
            gr, gi = parts[2 * m], parts[2 * m + 1]
            pr, pi = probe[m, 0], probe[m, 1]
            sum_r += pr * gr + pi * gi
            sum_i += pr * gi - pi * gr
            g_probe[m, 0] += wr * gr + wi * gi
            g_probe[m, 1] += wr * gi - wi * gr
        add_window(gext, 0, row, col, sum_r)
        add_window(gext, 1, row, col, sum_i)

    @pl.when(j == pl.num_programs(0) - 1)
    def _():
        flush(gext, (g_own, g_rgt, g_low, g_cor), sems, tile, size)


def on_device(obj_field, probe_modes, positions, counts, amplitudes):
    modes, _, _, size = probe_modes.shape
    tile = obj_field.shape[2]
    slots = amplitudes.shape[2]
    span = tile + size
    both = 2 * size
    prop, four = tables_for(size)
    cnt = counts.reshape(1)
    pos = positions.reshape(2 * slots)
    amp = amplitudes.reshape(slots, size, size)
    probe = lax.all_gather(probe_modes, "gx", axis=2, tiled=True)

    def halo(part):
        lower = shifted(part[:, :size, :], "gy", -1)
        rightward = shifted(part[:, :, :size], "gx", -1)
        corner = shifted(lower[:, :, :size], "gx", -1)
        return part, rightward, lower, corner

    first = halo(obj_field[0])
    after, _ = lax.optimization_barrier((obj_field[1], first[2]))
    second = halo(after)

    anywhere = pl.BlockSpec(memory_space=pl.ANY)
    per_slot = lambda *shape: pl.BlockSpec(
        (1,) + shape, lambda j, c, p: (jnp.minimum(j, c[0] - 1),) + (0,) * len(shape)
    )
    whole = lambda *shape: pl.BlockSpec(shape, lambda j, c, p: (0,) * len(shape))
    f32 = lambda *shape: jax.ShapeDtypeStruct(shape, jnp.float32)
    piece_shapes = (
        f32(2, tile, tile), f32(2, tile, size), f32(2, size, tile), f32(2, size, size)
    )
    ext = pltpu.VMEM((2, span, span), jnp.float32)
    sems = pltpu.SemaphoreType.DMA((4,))
    params = pltpu.CompilerParams(vmem_limit_bytes=VMEM_BYTES)
    wave_spec = per_slot(both, both)
    table_spec = whole(4, both, both)
    probe_spec = whole(modes, 2, size, size)
    work = 3 * 2 * 2 * both**3 * slots

    def call(kernel, in_specs, out_specs, out_shape, scratch, flops):
        return pl.pallas_call(
            functools.partial(kernel, tile, size),
            grid_spec=pltpu.PrefetchScalarGridSpec(
                num_scalar_prefetch=2,
                grid=(slots,),
                in_specs=in_specs,
                out_specs=out_specs,
                scratch_shapes=scratch,
            ),
            out_shape=out_shape,
            compiler_params=params,
            cost_estimate=pl.CostEstimate(
                flops=flops, bytes_accessed=16 * 1024 * 1024, transcendentals=0
            ),
        )

    wave = call(
        forward_kernel,
        [anywhere] * 4 + [probe_spec, table_spec],
        wave_spec,
        f32(slots, both, both),
        [ext, sems],
        work,
    )(cnt, pos, *first, probe, prop)
    gwave, *grads_1 = call(
        middle_kernel,
        [anywhere] * 4 + [wave_spec, per_slot(size, size), table_spec],
        [wave_spec] + [anywhere] * 4,
        (f32(slots, both, both),) + piece_shapes,
        [ext, ext, sems],
        2 * work,
    )(cnt, pos, *second, wave, amp, four)
    g_probe, *grads_0 = call(
        backward_kernel,
        [anywhere] * 4 + [wave_spec, probe_spec, table_spec],
        [probe_spec] + [anywhere] * 4,
        (f32(modes, 2, size, size),) + piece_shapes,
        [ext, ext, sems],
        work,
    )(cnt, pos, *first, gwave, probe, prop)

    def back(grads):
        own, rightward, lower, corner = grads
        corner = shifted(corner, "gx", 1)
        rightward = shifted(rightward, "gx", 1)
        lower = shifted(lower.at[:, :, :size].add(corner), "gy", 1)
        own = own.at[:, :, :size].add(rightward)
        return own.at[:, :size, :].add(lower)

    obj_grad = jnp.stack([back(grads_0), back(grads_1)])
    rows = lax.psum_scatter(g_probe, "gx", scatter_dimension=2, tiled=True)
    probe_grad = lax.psum(rows, "gy")
    return (obj_grad, probe_grad)


def solution(mesh):
    return jax.shard_map(
        on_device,
        mesh=mesh,
        in_specs=(
            P(None, None, "gy", "gx"),
            P(None, None, "gx", None),
            P("gy", "gx", None, None),
            P("gy", "gx"),
            P("gy", "gx", None, None, None),
        ),
        out_specs=(P(None, None, "gy", "gx"), P(None, None, "gx", None)),
        check_vma=False,
    )
```

time: 749 us -> 261 us (0.35)
  matrix products: 347 us -> 0 us
  local copies, waits for them, and re-layouts: 137 us -> 14.9 us
  Pallas kernels: 0 us -> 75.9 us
  other arithmetic: 55.7 us -> 10.4 us
  loops' own time: 33 us -> 0 us
  waiting for transfers between devices: 132 us -> 114 us
    dot_general x192 -> x0, matrix products: 347 us -> none  [the longest x24 54.9 us: left_apply(): jnp.einsum('ab,mbc->mac', mat_im, wave_im, precision=highest)]
    pallas_call x0 -> x3, Pallas kernels: none -> 75.9 us  [the longest x1 35 us: on_device(): call(middle_kernel, [anywhere] * 4 + [wave_spec, per_slot(size, size), ta...]
    dynamic_update_slice x6 -> x0, local copies, waits for them, and re-layouts: 71.3 us -> none  [visit(): grad_ext = lax.dynamic_update_slice(grad_ext, current + window_grad, starts)]
    another operation x1 -> x0, loops' own time: 33 us -> none  [on_device(): grad_ext, grad_probe = lax.fori_loop(0, slot_total, masked_visit, initial)]
    add x12 -> x0, other arithmetic: 29.2 us -> none  [the longest x6 16 us: visit(): return (grad_ext, grad_probe + modes_grad)]
    reduce_sum x24 -> x0, local copies, waits for them, and re-layouts: 21.4 us -> none  [the longest x12 15.6 us: position_loss(): wave_re = mode_set[:, 0] * window[0, 0] - mode_set[:, 1] * window[0, 1]]
    all_gather x1, waiting for transfers between devices: 21.3 us -> 0.02 us  [on_device(): probe = lax.all_gather(probe_modes, 'gx', axis=2, tiled=True)]
    psum x1, waiting for transfers between devices: 19.1 us -> 36.9 us  [on_device(): probe_grad = lax.psum(rows, 'gy')]
  transfers between devices with their start and end apart: 11 -> 15, of which waited for: 6 -> 7; matrix products, arithmetic and copies ran while one was open for 4% -> 7% of each run, Pallas kernels for 0% -> 16%
where the time goes in v1:
time: 261 us; the launch traced here: 258 us
  waiting for transfers between devices  114 us (44%)
  Pallas kernels  75.9 us (29%)
  starting transfers between devices  28.2 us (11%)
  local copies, waits for them, and re-layouts  14.9 us (6%)
  between operations  14.7 us (6%)
  other arithmetic  10.4 us (4%)
    ppermute x12, waiting for transfers between devices, shifted(): return lax.ppermute(x, axis, pairs)  77.3 us
    psum x1, waiting for transfers between devices, on_device(): probe_grad = lax.psum(rows, 'gy')  36.9 us
    pallas_call x1, Pallas kernels, on_device(): call(middle_kernel, [anywhere] * 4 + [wave_spec, per_slot(size, size), ta...  35 us
    ppermute x12, starting transfers between devices, shifted(): return lax.ppermute(x, axis, pairs)  28.1 us
    pallas_call x1, Pallas kernels, on_device(): call(backward_kernel, [anywhere] * 4 + [wave_spec, probe_spec, table_spec...  21.9 us
    pallas_call x1, Pallas kernels, on_device(): call(forward_kernel, [anywhere] * 4 + [probe_spec, table_spec], wave_spec...  19 us
    unnamed x18, local copies, waits for them, and re-layouts  5.27 us
  transfers between devices with their start and end apart: 15, of which 7 were waited for; matrix products, arithmetic and copies ran while one was open for 7% of the time, Pallas kernels for 16%

profile of v1, /device:TPU:20, one launch (start us, length us, event | category | flops | bytes accessed | tf_op | source)
XLA Modules:
  0.0 258.3 jit_solution(12931817677968908218)
XLA Ops:
  7.2 4.2 %slice_bitcast_fusion.1 = (f32[2,512,512]{2,1,0:T(8,128)S(1)}, f32[2,512,512]{2,1,0:T(8,128)}) fusion(f32[2,2,512,512]{3,2,1,0:T(8,128)} %param.19), kind=kLoop, calls=%fused_computation.2 | loop fusion | bytes 8388608 | tf_op jit(solution)/shard_map/squeeze | solution.py:270
  11.5 3.3 %collective-permute-start.1 = (f32[2,256,512]{2,1,0:T(8,128)S(1)}, f32[2,256,512]{2,1,0:T(8,128)}, u32[]{:S(2)}, u32[]{:S(2)}) collective-permute-start(f32[2,256,512]{2,1,0:T(8,128)S(1)} %slice.183), channel_id=1, source_target_pairs={{1,0},{2,1},{3,2},{5,4},{6,5},{7,6},{9,8},{10,9},{11,10},{13,12},{... | collective-permute-start | bytes 3145736 | tf_op jit(solution)/shard_map/ppermute | solution.py:21
  14.9 23.5 %collective-permute-done.1.low = f32[2,256,512]{2,1,0:T(8,128)} collective-permute-done((f32[2,256,512]{2,1,0:T(8,128)S(1)}, f32[2,256,512]{2,1,0:T(8,128)}, u32[]{:S(2)}, u32[]{:S(2)}) %collective-permute-start.1) | collective-permute-done | bytes 1048608 | tf_op jit(solution)/shard_map/ppermute | solution.py:21
  38.4 2.3 slice.174
  40.7 4.4 %collective-permute-start.4 = (f32[2,256,512]{2,1,0:T(8,128)}, f32[2,256,512]{2,1,0:T(8,128)}, u32[]{:S(2)}, u32[]{:S(2)}) collective-permute-start(f32[2,256,512]{2,1,0:T(8,128)} %slice.174), channel_id=1, source_target_pairs={{1,0},{2,1},{3,2},{5,4},{6,5},{7,6},{9,8},{10,9},{11,10},{13,12},{... | collective-permute-start | bytes 3145736 | tf_op jit(solution)/shard_map/ppermute | solution.py:21
  45.2 1.9 collective-permute-start
  47.1 1.1 slice.184
  48.2 2.5 collective-permute-start.2
  50.8 1.9 collective-permute-start.3
  54.1 12.9 %collective-permute-done.4.low = f32[2,256,512]{2,1,0:T(8,128)} collective-permute-done((f32[2,256,512]{2,1,0:T(8,128)}, f32[2,256,512]{2,1,0:T(8,128)}, u32[]{:S(2)}, u32[]{:S(2)}) %collective-permute-start.4) | collective-permute-done | bytes 1048608 | tf_op jit(solution)/shard_map/ppermute | solution.py:21
  68.1 1.9 collective-permute-start.5
  70.1 19.0 %shard_map.86.wave = f32[6,512,512]{2,1,0:T(8,128)} custom-call(s32[1]{0:T(128)} %bitcast.16.cnt, s32[12]{0:T(128)} %reshape.191.pos, f32[2,512,512]{2,1,0:T(8,128)} %copy-done.2, f32[2,512,256]{2,1,0:T(8,128)} %collective-permute-done.rgt, f32[2,256,512]{2,1,0:T(8,128)} %collective-permute-done.1.low, f32[2,256,256]{2,1,0:T(8,128)} %collective-permute-done.2.cor, ...), custom_call_target="tpu_custom_call" | custom-call | flops 9663676416 | bytes 16777216 | tf_op jit(solution)/shard_map/pallas_call | solution.py:308
  89.1 35.0 %shard_map.87 = (f32[6,512,512]{2,1,0:T(8,128)}, f32[2,512,512]{2,1,0:T(8,128)}, f32[2,512,256]{2,1,0:T(8,128)}, f32[2,256,512]{2,1,0:T(8,128)}, f32[2,256,256]{2,1,0:T(8,128)}) custom-call(s32[1]{0:T(128)} %bitcast.17.cnt, s32[12]{0:T(128)} %reshape.191.pos, f32[2,512,512]{2,1,0:T(8,128)} %get-tuple-element.85.own, ...), custom_call_target="tpu_custom_call" | custom-call | flops 19327352832 | bytes 16777216 | tf_op jit(solution)/shard_map/pallas_call | solution.py:316
  124.1 2.5 collective-permute-start.10
  126.6 1.9 collective-permute-start.9
  128.5 21.9 %shard_map.88 = (f32[2,2,256,256]{3,2,1,0:T(8,128)}, f32[2,512,512]{2,1,0:T(8,128)}, f32[2,512,256]{2,1,0:T(8,128)}, f32[2,256,512]{2,1,0:T(8,128)}, f32[2,256,256]{2,1,0:T(8,128)}) custom-call(s32[1]{0:T(128)} %bitcast.18.cnt, s32[12]{0:T(128)} %reshape.191.pos, f32[2,512,512]{2,1,0:T(8,128)} %copy-done.2, f32[2,512,256]{2,1,0:T(8,128)} %collective-permute-done.rgt, ...), custom_call_target="tpu_custom_call" | custom-call | flops 9663676416 | bytes 16777216 | tf_op jit(solution)/shard_map/pallas_call | solution.py:324
  150.4 1.9 collective-permute-start.7
  152.5 2.1 collective-permute-start.6
  154.5 2.1 add_dynamic-update-slice_fusion.2
  156.6 1.9 collective-permute-start.11
  158.6 4.2 %collective-permute-done.7 = f32[2,256,256]{2,1,0:T(8,128)} collective-permute-done((f32[2,256,256]{2,1,0:T(8,128)}, f32[2,256,256]{2,1,0:T(8,128)}, u32[]{:S(2)}, u32[]{:S(2)}) %collective-permute-start.7) | collective-permute-done | bytes 524320 | tf_op jit(solution)/shard_map/ppermute | solution.py:21
  162.7 2.1 add_dynamic-update-slice_fusion.3
  164.9 1.9 collective-permute-start.8
  167.3 14.8 %collective-permute-done.6 = f32[2,512,256]{2,1,0:T(8,128)S(1)} collective-permute-done((f32[2,512,256]{2,1,0:T(8,128)}, f32[2,512,256]{2,1,0:T(8,128)S(1)}, u32[]{:S(2)}, u32[]{:S(2)}) %collective-permute-start.6) | collective-permute-done | bytes 1048608 | tf_op jit(solution)/shard_map/ppermute | solution.py:21
  182.3 1.3 copy.16
  183.7 2.0 collective-permute-done.11
  185.9 1.3 copy-done.4
  187.2 20.0 %collective-permute-done.8 = f32[2,256,512]{2,1,0:T(8,128)S(1)} collective-permute-done((f32[2,256,512]{2,1,0:T(8,128)}, f32[2,256,512]{2,1,0:T(8,128)S(1)}, u32[]{:S(2)}, u32[]{:S(2)}) %collective-permute-start.8) | collective-permute-done | bytes 1048608 | tf_op jit(solution)/shard_map/ppermute | solution.py:21
  207.2 1.2 fusion.3
  209.1 4.2 %pad_maximum_fusion = f32[2,2,512,512]{3,2,1,0:T(8,128)} fusion(f32[1,2,512,512]{3,2,1,0:T(8,128)S(1)} %copy-done.5, f32[1,2,512,512]{3,2,1,0:T(8,128)} %fusion.3), kind=kLoop, calls=%fused_computation | loop fusion | flops 1048576 | bytes 8388608 | tf_op jit(solution)/shard_map/stack | solution.py:341
  213.4 36.9 %all-reduce.2.cloned.1.call-done = f32[2,2,32,256]{3,2,1,0:T(8,128)} async-done(((f32[2,2,32,256]{3,2,1,0:T(8,128)}), f32[2,2,32,256]{3,2,1,0:T(8,128)}) %all-reduce.2.cloned.1.call-update) | async-done | bytes 131088 | tf_op jit(solution)/shard_map/psum | solution.py:343
  250.2 1.6 copy.19
  (37 shorter events, 4.0 us)
Async XLA Ops:
  7.2 62.9 %all-gather.2.cloned.1.call-start = ((), (), s32[]{:S(2)}) async-start(), calls=%async_computation.1 | async-start | bytes 1179648 | tf_op jit(solution)/shard_map/all_gather | solution.py:262
  11.4 33.6 %copy-start.2 = (f32[2,512,512]{2,1,0:T(8,128)}, f32[2,512,512]{2,1,0:T(8,128)S(1)}, u32[]{:S(2)}) copy-start(f32[2,512,512]{2,1,0:T(8,128)S(1)} %get-tuple-element.96.own) | copy-start | bytes 6291460
  11.5 26.9 %collective-permute-start.1 = (f32[2,256,512]{2,1,0:T(8,128)S(1)}, f32[2,256,512]{2,1,0:T(8,128)}, u32[]{:S(2)}, u32[]{:S(2)}) collective-permute-start(f32[2,256,512]{2,1,0:T(8,128)S(1)} %slice.183), channel_id=1, source_target_pairs={{1,0},{2,1},{3,2},{5,4},{6,5},{7,6},{9,8},{10,9},{11,10},{13,12},{... | collective-permute-start | bytes 3145736 | tf_op jit(solution)/shard_map/ppermute | solution.py:21
  14.9 193.5 %reduce-scatter.2.cloned.1.call-start = ((), (), s32[]{:S(2)}) async-start(), calls=%async_computation.2 | async-start | bytes 1179648 | tf_op jit(solution)/shard_map/reduce_scatter | solution.py:342
  40.7 10.0 %copy-start.3 = (f32[2,512,512]{2,1,0:T(8,128)S(1)}, f32[2,512,512]{2,1,0:T(8,128)}, u32[]{:S(2)}) copy-start(f32[2,512,512]{2,1,0:T(8,128)} %get-tuple-element.85.own) | copy-start | bytes 6291460
  40.7 26.4 %collective-permute-start.4 = (f32[2,256,512]{2,1,0:T(8,128)}, f32[2,256,512]{2,1,0:T(8,128)}, u32[]{:S(2)}, u32[]{:S(2)}) collective-permute-start(f32[2,256,512]{2,1,0:T(8,128)} %slice.174), channel_id=1, source_target_pairs={{1,0},{2,1},{3,2},{5,4},{6,5},{7,6},{9,8},{10,9},{11,10},{13,12},{... | collective-permute-start | bytes 3145736 | tf_op jit(solution)/shard_map/ppermute | solution.py:21
  45.2 8.2 %copy-start.6 = (s32[1,1,6,2]{2,3,1,0:T(2,128)S(1)}, s32[1,1,6,2]{2,3,1,0:T(2,128)}, u32[]{:S(2)}) copy-start(s32[1,1,6,2]{2,3,1,0:T(2,128)} %param.21) | copy-start | bytes 148
  45.2 24.9 %collective-permute-start = (f32[2,512,256]{2,1,0:T(8,128)S(1)}, f32[2,512,256]{2,1,0:T(8,128)}, u32[]{:S(2)}, u32[]{:S(2)}) collective-permute-start(f32[2,512,256]{2,1,0:T(8,128)S(1)} %slice.182), channel_id=1, source_target_pairs={{4,0},{8,4},{12,8},{16,12},{20,16},{24,20},{28,24},{5,1},{9,5},{13... | collective-permute-start | bytes 3145736 | tf_op jit(solution)/shard_map/ppermute | solution.py:21
  48.2 21.9 %collective-permute-start.2 = (f32[2,256,256]{2,1,0:T(8,128)S(1)}, f32[2,256,256]{2,1,0:T(8,128)}, u32[]{:S(2)}, u32[]{:S(2)}) collective-permute-start(f32[2,256,256]{2,1,0:T(8,128)S(1)} %slice.184), channel_id=1, source_target_pairs={{4,0},{8,4},{12,8},{16,12},{20,16},{24,20},{28,24},{5,1},{9,5},{13... | collective-permute-start | bytes 1572872 | tf_op jit(solution)/shard_map/ppermute | solution.py:21
  50.8 38.3 %collective-permute-start.3 = (f32[2,512,256]{2,1,0:T(8,128)S(1)}, f32[2,512,256]{2,1,0:T(8,128)}, u32[]{:S(2)}, u32[]{:S(2)}) collective-permute-start(f32[2,512,256]{2,1,0:T(8,128)S(1)} %slice.173), channel_id=1, source_target_pairs={{4,0},{8,4},{12,8},{16,12},{20,16},{24,20},{28,24},{5,1},{9,5},{13... | collective-permute-start | bytes 3145736 | tf_op jit(solution)/shard_map/ppermute | solution.py:21
  68.1 21.0 %collective-permute-start.5 = (f32[2,256,256]{2,1,0:T(8,128)S(1)}, f32[2,256,256]{2,1,0:T(8,128)}, u32[]{:S(2)}, u32[]{:S(2)}) collective-permute-start(f32[2,256,256]{2,1,0:T(8,128)S(1)} %slice.185), channel_id=1, source_target_pairs={{4,0},{8,4},{12,8},{16,12},{20,16},{24,20},{28,24},{5,1},{9,5},{13... | collective-permute-start | bytes 1572872 | tf_op jit(solution)/shard_map/ppermute | solution.py:21
  124.1 30.4 %collective-permute-start.10 = (f32[2,256,256]{2,1,0:T(8,128)}, f32[2,256,256]{2,1,0:T(8,128)}, u32[]{:S(2)}, u32[]{:S(2)}) collective-permute-start(f32[2,256,256]{2,1,0:T(8,128)} %get-tuple-element.94), channel_id=1, source_target_pairs={{0,4},{4,8},{8,12},{12,16},{16,20},{20,24},{24,28},{1,5},{5,9},{9,... | collective-permute-start | bytes 1572872 | tf_op jit(solution)/shard_map/ppermute | solution.py:21
  126.6 40.2 %collective-permute-start.9 = (f32[2,512,256]{2,1,0:T(8,128)}, f32[2,512,256]{2,1,0:T(8,128)S(1)}, u32[]{:S(2)}, u32[]{:S(2)}) collective-permute-start(f32[2,512,256]{2,1,0:T(8,128)} %get-tuple-element.92), channel_id=1, source_target_pairs={{0,4},{4,8},{8,12},{12,16},{16,20},{20,24},{24,28},{1,5},{5,9},{9,... | collective-permute-start | bytes 3145736 | tf_op jit(solution)/shard_map/ppermute | solution.py:21
  150.4 12.3 %collective-permute-start.7 = (f32[2,256,256]{2,1,0:T(8,128)}, f32[2,256,256]{2,1,0:T(8,128)}, u32[]{:S(2)}, u32[]{:S(2)}) collective-permute-start(f32[2,256,256]{2,1,0:T(8,128)} %get-tuple-element.90), channel_id=1, source_target_pairs={{0,4},{4,8},{8,12},{12,16},{16,20},{20,24},{24,28},{1,5},{5,9},{9,... | collective-permute-start | bytes 1572872 | tf_op jit(solution)/shard_map/ppermute | solution.py:21
  152.4 14.4 %copy-start = (f32[2,512,512]{2,1,0:T(8,128)S(1)}, f32[2,512,512]{2,1,0:T(8,128)}, u32[]{:S(2)}) copy-start(f32[2,512,512]{2,1,0:T(8,128)} %get-tuple-element.91) | copy-start | bytes 6291460
  152.4 97.8 %all-reduce.2.cloned.1.call-start = ((), (), s32[]{:S(2)}) async-start(), calls=%async_computation.3 | async-start | bytes 262144 | tf_op jit(solution)/shard_map/psum | solution.py:343
  152.5 29.6 %collective-permute-start.6 = (f32[2,512,256]{2,1,0:T(8,128)}, f32[2,512,256]{2,1,0:T(8,128)S(1)}, u32[]{:S(2)}, u32[]{:S(2)}) collective-permute-start(f32[2,512,256]{2,1,0:T(8,128)} %get-tuple-element.88), channel_id=1, source_target_pairs={{0,4},{4,8},{8,12},{12,16},{16,20},{20,24},{24,28},{1,5},{5,9},{9,... | collective-permute-start | bytes 3145736 | tf_op jit(solution)/shard_map/ppermute | solution.py:21
  156.6 29.0 %collective-permute-start.11 = (f32[2,256,512]{2,1,0:T(8,128)}, f32[2,256,512]{2,1,0:T(8,128)S(1)}, u32[]{:S(2)}, u32[]{:S(2)}) collective-permute-start(f32[2,256,512]{2,1,0:T(8,128)} %add_dynamic-update-slice_fusion.2), channel_id=1, source_target_pairs={{0,1},{1,2},{2,3},{4,5},{5,6},{6,7},{8,9},{9,10},{10,11},{12,13},{... | collective-permute-start | bytes 3145736 | tf_op jit(solution)/shard_map/ppermute | solution.py:21
  164.9 42.3 %collective-permute-start.8 = (f32[2,256,512]{2,1,0:T(8,128)}, f32[2,256,512]{2,1,0:T(8,128)S(1)}, u32[]{:S(2)}, u32[]{:S(2)}) collective-permute-start(f32[2,256,512]{2,1,0:T(8,128)} %add_dynamic-update-slice_fusion.3), channel_id=1, source_target_pairs={{0,1},{1,2},{2,3},{4,5},{5,6},{6,7},{8,9},{9,10},{10,11},{12,13},{... | collective-permute-start | bytes 3145736 | tf_op jit(solution)/shard_map/ppermute | solution.py:21
  167.1 15.0 %copy-start.1 = (f32[2,512,512]{2,1,0:T(8,128)S(1)}, f32[2,512,512]{2,1,0:T(8,128)}, u32[]{:S(2)}) copy-start(f32[2,512,512]{2,1,0:T(8,128)} %get-tuple-element.87) | copy-start | bytes 6291460
  185.9 1.3 copy-start.4
  207.2 2.0 copy-start.5
Sparse Core Ops, SparseCore 0:
  15.0 22.7 all-gather.1
  152.5 26.6 reduce-scatter.1
  208.5 41.6 all-reduce.1

commit v2 on v1

--- a/solution.py
+++ b/solution.py
@@ -121,19 +121,23 @@
     ext[plane, pl.ds(top, size + ROWS), pl.ds(base, size + LANES)] += wide
 
 
-def regions(ext, tile, size):
-    return (
+def regions(ext, count, tile, size):
+    whole = [
         ext.at[:, pl.ds(0, tile), pl.ds(0, tile)],
         ext.at[:, pl.ds(0, tile), pl.ds(tile, size)],
+    ]
+    if count == 3:
+        return whole + [ext.at[:, pl.ds(tile, size), :]]
+    return whole + [
         ext.at[:, pl.ds(tile, size), pl.ds(0, tile)],
         ext.at[:, pl.ds(tile, size), pl.ds(tile, size)],
-    )
-
-
-def fetch(pieces, ext, sems, tile, size):
+    ]
+
+
+def run_copies(sources, targets, sems):
     copies = [
-        pltpu.make_async_copy(piece, region, sems.at[k])
-        for k, (piece, region) in enumerate(zip(pieces, regions(ext, tile, size)))
+        pltpu.make_async_copy(source, target, sems.at[k])
+        for k, (source, target) in enumerate(zip(sources, targets))
     ]
     for copy in copies:
         copy.start()
@@ -141,23 +145,20 @@
         copy.wait()
 
 
+def fetch(pieces, ext, sems, tile, size):
+    run_copies(pieces, regions(ext, len(pieces), tile, size), sems)
+
+
 def flush(ext, pieces, sems, tile, size):
-    copies = [
-        pltpu.make_async_copy(region, piece, sems.at[k])
-        for k, (piece, region) in enumerate(zip(pieces, regions(ext, tile, size)))
-    ]
-    for copy in copies:
-        copy.start()
-    for copy in copies:
-        copy.wait()
-
-
-def forward_kernel(tile, size, cnt, pos, own, rgt, low, cor, probe, table, out, ext, sems):
+    run_copies(regions(ext, len(pieces), tile, size), pieces, sems)
+
+
+def forward_kernel(tile, size, cnt, pos, obj, rgt, low, cor, probe, table, out, ext, sems):
     j = pl.program_id(0)
 
     @pl.when(j == 0)
     def _():
-        fetch((own, rgt, low, cor), ext, sems, tile, size)
+        fetch((obj.at[0], rgt, low, cor), ext, sems, tile, size)
 
     @pl.when(j < cnt[0])
     def _():
@@ -173,14 +174,14 @@
 
 
 def middle_kernel(
-    tile, size, cnt, pos, own, rgt, low, cor, wave, amp, table,
-    gwave, g_own, g_rgt, g_low, g_cor, ext, gext, sems,
+    tile, size, cnt, pos, obj, rgt, bot, wave, amp, table,
+    gwave, g_obj, g_rgt, g_bot, ext, gext, sems,
 ):
     j = pl.program_id(0)
 
     @pl.when(j == 0)
     def _():
-        fetch((own, rgt, low, cor), ext, sems, tile, size)
+        fetch((obj.at[1], rgt, bot), ext, sems, tile, size)
         gext[...] = jnp.zeros_like(gext)
 
     @pl.when(j < cnt[0])
@@ -210,18 +211,18 @@
 
     @pl.when(j == pl.num_programs(0) - 1)
     def _():
-        flush(gext, (g_own, g_rgt, g_low, g_cor), sems, tile, size)
+        flush(gext, (g_obj.at[1], g_rgt, g_bot), sems, tile, size)
 
 
 def backward_kernel(
-    tile, size, cnt, pos, own, rgt, low, cor, gwave, probe, table,
-    g_probe, g_own, g_rgt, g_low, g_cor, ext, gext, sems,
+    tile, size, cnt, pos, obj, rgt, low, cor, gwave, probe, table, _,
+    g_probe, g_obj, g_rgt, g_low, g_cor, ext, gext, sems,
 ):
     j = pl.program_id(0)
 
     @pl.when(j == 0)
     def _():
-        fetch((own, rgt, low, cor), ext, sems, tile, size)
+        fetch((obj.at[0], rgt, low, cor), ext, sems, tile, size)
         gext[...] = jnp.zeros_like(gext)
         g_probe[...] = jnp.zeros_like(g_probe)
 
@@ -246,7 +247,36 @@
 
     @pl.when(j == pl.num_programs(0) - 1)
     def _():
-        flush(gext, (g_own, g_rgt, g_low, g_cor), sems, tile, size)
+        flush(gext, (g_obj.at[0], g_rgt, g_low, g_cor), sems, tile, size)
+
+
+def partners(axis, bit):
+    return [(i, i ^ (1 << bit)) for i in range(lax.axis_size(axis))]
+
+
+def scattered_rows(x, axis):
+    n = lax.axis_size(axis)
+    if n & (n - 1):
+        return lax.psum_scatter(x, axis, scatter_dimension=2, tiled=True)
+    bits = n.bit_length() - 1
+    me = lax.axis_index(axis)
+    x = x.reshape(x.shape[:2] + (2,) * bits + (x.shape[2] // n, x.shape[3]))
+    for bit in range(bits):
+        dim = 2 + bits - 1 - bit
+        mine = (me >> bit) & 1
+        kept = lax.dynamic_index_in_dim(x, mine, dim, keepdims=False)
+        sent = lax.dynamic_index_in_dim(x, 1 - mine, dim, keepdims=False)
+        x = kept + lax.ppermute(sent, axis, partners(axis, bit))
+    return x
+
+
+def summed(x, axis):
+    n = lax.axis_size(axis)
+    if n & (n - 1):
+        return lax.psum(x, axis)
+    for bit in range(n.bit_length() - 1):
+        x = x + lax.ppermute(x, axis, partners(axis, bit))
+    return x
 
 
 def on_device(obj_field, probe_modes, positions, counts, amplitudes):
@@ -261,15 +291,13 @@
     amp = amplitudes.reshape(slots, size, size)
     probe = lax.all_gather(probe_modes, "gx", axis=2, tiled=True)
 
-    def halo(part):
-        lower = shifted(part[:, :size, :], "gy", -1)
-        rightward = shifted(part[:, :, :size], "gx", -1)
-        corner = shifted(lower[:, :, :size], "gx", -1)
-        return part, rightward, lower, corner
-
-    first = halo(obj_field[0])
-    after, _ = lax.optimization_barrier((obj_field[1], first[2]))
-    second = halo(after)
+    lower = shifted(obj_field[0, :, :size, :], "gy", -1)
+    rightward = shifted(obj_field[0, :, :, :size], "gx", -1)
+    right_1 = shifted(obj_field[1, :, :, :size], "gx", -1)
+    corner = shifted(lower[:, :, :size], "gx", -1)
+    bottom = jnp.concatenate([obj_field[1, :, :size, :], right_1[:, :size, :]], axis=2)
+    bottom, lower = lax.optimization_barrier((bottom, lower))
+    bottom = shifted(bottom, "gy", -1)
 
     anywhere = pl.BlockSpec(memory_space=pl.ANY)
     per_slot = lambda *shape: pl.BlockSpec(
@@ -277,9 +305,8 @@
     )
     whole = lambda *shape: pl.BlockSpec(shape, lambda j, c, p: (0,) * len(shape))
     f32 = lambda *shape: jax.ShapeDtypeStruct(shape, jnp.float32)
-    piece_shapes = (
-        f32(2, tile, tile), f32(2, tile, size), f32(2, size, tile), f32(2, size, size)
-    )
+    obj_shape = f32(*obj_field.shape)
+    right_shape = f32(2, tile, size)
     ext = pltpu.VMEM((2, span, span), jnp.float32)
     sems = pltpu.SemaphoreType.DMA((4,))
     params = pltpu.CompilerParams(vmem_limit_bytes=VMEM_BYTES)
@@ -288,7 +315,7 @@
     probe_spec = whole(modes, 2, size, size)
     work = 3 * 2 * 2 * both**3 * slots
 
-    def call(kernel, in_specs, out_specs, out_shape, scratch, flops):
+    def call(kernel, in_specs, out_specs, out_shape, scratch, flops, aliases):
         return pl.pallas_call(
             functools.partial(kernel, tile, size),
             grid_spec=pltpu.PrefetchScalarGridSpec(
@@ -299,6 +326,7 @@
                 scratch_shapes=scratch,
             ),
             out_shape=out_shape,
+            input_output_aliases=aliases,
             compiler_params=params,
             cost_estimate=pl.CostEstimate(
                 flops=flops, bytes_accessed=16 * 1024 * 1024, transcendentals=0
@@ -312,36 +340,40 @@
         f32(slots, both, both),
         [ext, sems],
         work,
-    )(cnt, pos, *first, probe, prop)
-    gwave, *grads_1 = call(
+        {},
+    )(cnt, pos, obj_field, rightward, lower, corner, probe, prop)
+    gwave, g_obj, g_right_1, g_bottom = call(
         middle_kernel,
-        [anywhere] * 4 + [wave_spec, per_slot(size, size), table_spec],
-        [wave_spec] + [anywhere] * 4,
-        (f32(slots, both, both),) + piece_shapes,
+        [anywhere] * 3 + [wave_spec, per_slot(size, size), table_spec],
+        [wave_spec] + [anywhere] * 3,
+        (f32(slots, both, both), obj_shape, right_shape, f32(2, size, span)),
         [ext, ext, sems],
         2 * work,
-    )(cnt, pos, *second, wave, amp, four)
-    g_probe, *grads_0 = call(
+        {},
+    )(cnt, pos, obj_field, right_1, bottom, wave, amp, four)
+    g_bottom = shifted(g_bottom, "gy", 1)
+    g_right_1 = shifted(g_right_1, "gx", 1)
+    g_probe, g_obj, g_right, g_lower, g_corner = call(
         backward_kernel,
-        [anywhere] * 4 + [wave_spec, probe_spec, table_spec],
+        [anywhere] * 4 + [wave_spec, probe_spec, table_spec, anywhere],
         [probe_spec] + [anywhere] * 4,
-        (f32(modes, 2, size, size),) + piece_shapes,
+        (f32(modes, 2, size, size), obj_shape, right_shape, f32(2, size, tile), f32(2, size, size)),
         [ext, ext, sems],
         work,
-    )(cnt, pos, *first, gwave, probe, prop)
-
-    def back(grads):
-        own, rightward, lower, corner = grads
-        corner = shifted(corner, "gx", 1)
-        rightward = shifted(rightward, "gx", 1)
-        lower = shifted(lower.at[:, :, :size].add(corner), "gy", 1)
-        own = own.at[:, :, :size].add(rightward)
-        return own.at[:, :size, :].add(lower)
-
-    obj_grad = jnp.stack([back(grads_0), back(grads_1)])
-    rows = lax.psum_scatter(g_probe, "gx", scatter_dimension=2, tiled=True)
-    probe_grad = lax.psum(rows, "gy")
-    return (obj_grad, probe_grad)
+        {9: 1},
+    )(cnt, pos, obj_field, rightward, lower, corner, gwave, probe, prop, g_obj)
+
+    g_corner = shifted(g_corner, "gx", 1)
+    g_lower = shifted(g_lower.at[:, :, :size].add(g_corner), "gy", 1)
+    g_right = shifted(g_right, "gx", 1)
+    g_corner_1 = shifted(g_bottom[:, :, tile:], "gx", 1)
+    probe_grad = summed(scattered_rows(g_probe, "gx"), "gy")
+    g_obj = g_obj.at[1, :, :, :size].add(g_right_1)
+    g_obj = g_obj.at[1, :, :size, :].add(g_bottom[:, :, :tile])
+    g_obj = g_obj.at[0, :, :, :size].add(g_right)
+    g_obj = g_obj.at[1, :, :size, :size].add(g_corner_1)
+    g_obj = g_obj.at[0, :, :size, :].add(g_lower)
+    return (g_obj, probe_grad)
 
 
 def solution(mesh):

time: 261 us -> 228 us (0.87)
  waiting for transfers between devices: 114 us -> 82.3 us
  local copies, waits for them, and re-layouts: 14.9 us -> 6.41 us
  other arithmetic: 10.4 us -> 15.4 us
  starting transfers between devices: 28.2 us -> 31.5 us
    psum x1 -> x0, waiting for transfers between devices: 36.9 us -> none  [on_device(): probe_grad = lax.psum(rows, 'gy')]
    ppermute x0 -> x5, waiting for transfers between devices: none -> 34.5 us  [the longest x2 26.4 us: summed(): x = x + lax.ppermute(x, axis, partners(axis, bit))]
    ppermute x12 -> x11, waiting for transfers between devices: 77.3 us -> 47.8 us  [shifted(): return lax.ppermute(x, axis, pairs)]
    scatter-add x6, other arithmetic: 6.16 us -> 13.4 us  [the longest x1 2.4 us: on_device(): g_obj = g_obj.at[0, :, :size, :].add(g_lower)]
    ppermute x0 -> x5, starting transfers between devices: none -> 5.93 us  [the longest x2 4 us: summed(): x = x + lax.ppermute(x, axis, partners(axis, bit))]
    slice x6 -> x3, local copies, waits for them, and re-layouts: 4.72 us -> 0.11 us  [the longest x1 0.04 us: on_device(): corner = shifted(lower[:, :, :size], 'gx', -1)]
    unnamed x18 -> x7, local copies, waits for them, and re-layouts: 5.27 us -> 1.03 us
    another operation x1 -> x0, other arithmetic: 4.22 us -> none  [on_device(): obj_grad = jnp.stack([back(grads_0), back(grads_1)])]
  transfers between devices with their start and end apart: 15 -> 17, of which waited for: 7 -> 10; matrix products, arithmetic and copies ran while one was open for 7% -> 7% of each run, Pallas kernels for 16% -> 8%
where the time goes in v2:
time: 228 us; the launch traced here: 227 us
  waiting for transfers between devices  82.3 us (36%)
  Pallas kernels  76 us (33%)
  starting transfers between devices  31.5 us (14%)
  other arithmetic  15.4 us (7%)
  between operations  15 us (7%)
  local copies, waits for them, and re-layouts  6.41 us (3%)
    ppermute x11, waiting for transfers between devices, shifted(): return lax.ppermute(x, axis, pairs)  47.8 us
    pallas_call x1, Pallas kernels, on_device(): call(middle_kernel, [anywhere] * 3 + [wave_spec, per_slot(size, size), ta...  35 us
    ppermute x2, waiting for transfers between devices, summed(): x = x + lax.ppermute(x, axis, partners(axis, bit))  26.4 us
    ppermute x11, starting transfers between devices, shifted(): return lax.ppermute(x, axis, pairs)  25.5 us
    pallas_call x1, Pallas kernels, on_device(): call(backward_kernel, [anywhere] * 4 + [wave_spec, probe_spec, table_spec...  22 us
    pallas_call x1, Pallas kernels, on_device(): call(forward_kernel, [anywhere] * 4 + [probe_spec, table_spec], wave_spec...  19 us
    ppermute x3, waiting for transfers between devices, scattered_rows(): x = kept + lax.ppermute(sent, axis, partners(axis, bit))  8.12 us
  transfers between devices with their start and end apart: 17, of which 10 were waited for; matrix products, arithmetic and copies ran while one was open for 7% of the time, Pallas kernels for 8%

profile of v2, /device:TPU:20, one launch (start us, length us, event | category | flops | bytes accessed | tf_op | source)
XLA Modules:
  0.0 226.6 jit_solution(6040909862103930098)
XLA Ops:
  8.9 1.9 collective-permute-start.1
  12.6 3.3 %collective-permute-start.2 = (f32[2,256,512]{2,1,0:T(8,128)S(1)}, f32[2,256,512]{2,1,0:T(8,128)S(1)}, u32[]{:S(2)}, u32[]{:S(2)}) collective-permute-start(f32[2,256,512]{2,1,0:T(8,128)S(1)} %get-tuple-element.96), channel_id=1, source_target_pairs={{1,0},{2,1},{3,2},{5,4},{6,5},{7,6},{9,8},{10,9},{11,10},{13,12},{... | collective-permute-start | bytes 3145736 | tf_op jit(solution)/shard_map/ppermute | solution.py:21
  16.0 2.2 collective-permute-start
  18.2 9.5 %collective-permute-done.1.rgt = f32[2,512,256]{2,1,0:T(8,128)S(1)} collective-permute-done((f32[2,512,256]{2,1,0:T(8,128)S(1)}, f32[2,512,256]{2,1,0:T(8,128)S(1)}, u32[]{:S(2)}, u32[]{:S(2)}) %collective-permute-start.1) | collective-permute-done | bytes 1048608 | tf_op jit(solution)/shard_map/ppermute | solution.py:21
  28.8 11.3 %collective-permute-done.2.low = f32[2,256,512]{2,1,0:T(8,128)S(1)} collective-permute-done((f32[2,256,512]{2,1,0:T(8,128)S(1)}, f32[2,256,512]{2,1,0:T(8,128)S(1)}, u32[]{:S(2)}, u32[]{:S(2)}) %collective-permute-start.2) | collective-permute-done | bytes 1048608 | tf_op jit(solution)/shard_map/ppermute | solution.py:21
  40.1 4.2 %collective-permute-start.4 = (f32[2,256,768]{2,1,0:T(8,128)S(1)}, f32[2,256,768]{2,1,0:T(8,128)}, u32[]{:S(2)}, u32[]{:S(2)}) collective-permute-start(f32[2,256,768]{2,1,0:T(8,128)S(1)} %pad_maximum_fusion), channel_id=1, source_target_pairs={{1,0},{2,1},{3,2},{5,4},{6,5},{7,6},{9,8},{10,9},{11,10},{13,12},{... | collective-permute-start | bytes 4718600 | tf_op jit(solution)/shard_map/ppermute | solution.py:21
  44.4 1.9 collective-permute-start.3
  47.7 5.2 %collective-permute-done.3.cor = f32[2,256,256]{2,1,0:T(8,128)} collective-permute-done((f32[2,256,256]{2,1,0:T(8,128)S(1)}, f32[2,256,256]{2,1,0:T(8,128)}, u32[]{:S(2)}, u32[]{:S(2)}) %collective-permute-start.3) | collective-permute-done | bytes 524320 | tf_op jit(solution)/shard_map/ppermute | solution.py:21
  53.0 19.0 %shard_map.86.wave = f32[6,512,512]{2,1,0:T(8,128)} custom-call(s32[1]{0:T(128)} %bitcast.40.cnt, s32[12]{0:T(128)} %reshape.246.pos, f32[2,2,512,512]{3,2,1,0:T(8,128)} %obj.5, f32[2,512,256]{2,1,0:T(8,128)} %collective-permute-done.rgt, f32[2,256,512]{2,1,0:T(8,128)} %copy-done.1, f32[2,256,256]{2,1,0:T(8,128)} %collective-permute-done.3.cor, ...), custom_call_target="tpu_custom_call" | custom-call | flops 9663676416 | bytes 16777216 | tf_op jit(solution)/shard_map/pallas_call | solution.py:336
  72.0 6.1 %collective-permute-done.4.bot = f32[2,256,768]{2,1,0:T(8,128)} collective-permute-done((f32[2,256,768]{2,1,0:T(8,128)S(1)}, f32[2,256,768]{2,1,0:T(8,128)}, u32[]{:S(2)}, u32[]{:S(2)}) %collective-permute-start.4) | collective-permute-done | bytes 1572896 | tf_op jit(solution)/shard_map/ppermute | solution.py:21
  78.1 35.0 %shard_map.87 = (f32[6,512,512]{2,1,0:T(8,128)}, f32[2,2,512,512]{3,2,1,0:T(8,128)}, f32[2,512,256]{2,1,0:T(8,128)}, f32[2,256,768]{2,1,0:T(8,128)}) custom-call(s32[1]{0:T(128)} %bitcast.41.cnt, s32[12]{0:T(128)} %reshape.246.pos, f32[2,2,512,512]{3,2,1,0:T(8,128)} %obj.5, f32[2,512,256]{2,1,0:T(8,128)} %copy-done, ...), custom_call_target="tpu_custom_call" | custom-call | flops 19327352832 | bytes 16777216 | tf_op jit(solution)/shard_map/pallas_call | solution.py:345
  113.1 22.0 %shard_map.88 = (f32[2,2,256,256]{3,2,1,0:T(8,128)}, f32[2,2,512,512]{3,2,1,0:T(8,128)}, f32[2,512,256]{2,1,0:T(8,128)}, f32[2,256,512]{2,1,0:T(8,128)}, f32[2,256,256]{2,1,0:T(8,128)}) custom-call(s32[1]{0:T(128)} %bitcast.42.cnt, s32[12]{0:T(128)} %reshape.246.pos, f32[2,2,512,512]{3,2,1,0:T(8,128)} %obj.5, ...), custom_call_target="tpu_custom_call", output_to_operand_aliasing={{1}: (9, {})} | custom-call | flops 9663676416 | bytes 16777216 | tf_op jit(solution)/shard_map/pallas_call | solution.py:356
  136.3 1.9 collective-permute-start.6
  139.5 1.8 collective-permute-start.12
  141.3 2.1 collective-permute-start.5
  143.4 2.1 collective-permute-start.9
  145.5 2.7 %collective-permute-done.12 = f32[2,2,2,32,256]{4,3,1,0,2:T(8,128)S(1)} collective-permute-done((f32[2,2,2,32,256]{4,3,1,0,2:T(8,128)S(1)}, f32[2,2,2,32,256]{4,3,1,0,2:T(8,128)S(1)}, u32[]{:S(2)}, u32[]{:S(2)}) %collective-permute-start.12) | collective-permute-done | bytes 262176 | tf_op jit(solution)/shard_map/ppermute | solution.py:269
  148.4 1.9 collective-permute-start.7
  150.3 5.4 %collective-permute-done.13 = f32[2,2,32,256]{3,2,1,0:T(8,128)S(1)} collective-permute-done((f32[2,2,32,256]{3,2,1,0:T(8,128)S(1)}, f32[2,2,32,256]{3,2,1,0:T(8,128)S(1)}, u32[]{:S(2)}, u32[]{:S(2)}) %collective-permute-start.13) | collective-permute-done | bytes 131104 | tf_op jit(solution)/shard_map/ppermute | solution.py:269
  155.8 11.7 %collective-permute-done.9 = f32[2,256,256]{2,1,0:T(8,128)} collective-permute-done((f32[2,256,256]{2,1,0:T(8,128)}, f32[2,256,256]{2,1,0:T(8,128)}, u32[]{:S(2)}, u32[]{:S(2)}) %collective-permute-start.9) | collective-permute-done | bytes 524320 | tf_op jit(solution)/shard_map/ppermute | solution.py:21
  167.5 2.1 add_dynamic-update-slice_fusion
  169.6 1.9 collective-permute-start.10
  171.5 4.5 %collective-permute-done.14 = f32[2,2,32,256]{3,2,1,0:T(8,128)S(1)} collective-permute-done((f32[2,2,32,256]{3,2,1,0:T(8,128)S(1)}, f32[2,2,32,256]{3,2,1,0:T(8,128)S(1)}, u32[]{:S(2)}, u32[]{:S(2)}) %collective-permute-start.14) | collective-permute-done | bytes 131104 | tf_op jit(solution)/shard_map/ppermute | solution.py:278
  176.0 3.9 %collective-permute-start.15 = (f32[2,2,32,256]{3,2,1,0:T(8,128)S(1)}, f32[2,2,32,256]{3,2,1,0:T(8,128)S(1)}, u32[]{:S(2)}, u32[]{:S(2)}) collective-permute-start(f32[2,2,32,256]{3,2,1,0:T(8,128)S(1)} %add.96), channel_id=1, source_target_pairs={{0,2},{1,3},{2,0},{3,1},{4,6},{5,7},{6,4},{7,5},{8,10},{9,11},{10,... | collective-permute-start | bytes 393224 | tf_op jit(solution)/shard_map/ppermute | solution.py:278
  180.0 2.3 %fusion.4 = f32[2,2,512,512]{3,2,1,0:T(8,128)} fusion(f32[2,2,512,512]{3,2,1,0:T(8,128)} %get-tuple-element.89, f32[2,512,256]{2,1,0:T(8,128)S(1)} %collective-permute-done.5), kind=kLoop, calls=%fused_computation.9 | loop fusion | flops 262144 | bytes 3145728 | tf_op jit(solution)/shard_map/scatter-add | solution.py:371
  182.3 21.9 %collective-permute-done.15 = f32[2,2,32,256]{3,2,1,0:T(8,128)S(1)} collective-permute-done((f32[2,2,32,256]{3,2,1,0:T(8,128)S(1)}, f32[2,2,32,256]{3,2,1,0:T(8,128)S(1)}, u32[]{:S(2)}, u32[]{:S(2)}) %collective-permute-start.15) | collective-permute-done | bytes 131104 | tf_op jit(solution)/shard_map/ppermute | solution.py:278
  204.9 1.9 collective-permute-start.8
  206.8 2.4 %fusion.3 = f32[2,2,512,512]{3,2,1,0:T(8,128)} fusion(f32[2,2,512,512]{3,2,1,0:T(8,128)} %fusion.4, f32[2,256,768]{2,1,0:T(8,128)S(1)} %collective-permute-done.6), kind=kLoop, calls=%fused_computation.7 | loop fusion | flops 262144 | bytes 3145728 | tf_op jit(solution)/shard_map/scatter-add | solution.py:372
  209.2 2.3 %fusion.1 = f32[2,2,512,512]{3,2,1,0:T(8,128)} fusion(f32[2,2,512,512]{3,2,1,0:T(8,128)} %fusion.3, f32[2,512,256]{2,1,0:T(8,128)S(1)} %collective-permute-done.7), kind=kLoop, calls=%fused_computation.4 | loop fusion | flops 262144 | bytes 3145728 | tf_op jit(solution)/shard_map/scatter-add | solution.py:373
  211.5 3.9 %collective-permute-done.8 = f32[2,256,256]{2,1,0:T(8,128)S(1)} collective-permute-done((f32[2,256,256]{2,1,0:T(8,128)S(1)}, f32[2,256,256]{2,1,0:T(8,128)S(1)}, u32[]{:S(2)}, u32[]{:S(2)}) %collective-permute-start.8) | collective-permute-done | bytes 524320 | tf_op jit(solution)/shard_map/ppermute | solution.py:21
  215.4 1.9 fusion.5
  217.3 2.4 %fusion = f32[2,2,512,512]{3,2,1,0:T(8,128)} fusion(f32[2,2,512,512]{3,2,1,0:T(8,128)} %fusion.5, f32[2,256,512]{2,1,0:T(8,128)S(1)} %collective-permute-done.10), kind=kLoop, calls=%fused_computation.2 | loop fusion | flops 262144 | bytes 3145728 | tf_op jit(solution)/shard_map/scatter-add | solution.py:375
  (35 shorter events, 8.7 us)
Async XLA Ops:
  7.2 45.8 %all-gather.2.cloned.1.call-start = ((), (), s32[]{:S(2)}) async-start(), calls=%async_computation | async-start | bytes 1179648 | tf_op jit(solution)/shard_map/all_gather | solution.py:292
  8.9 18.8 %collective-permute-start.1 = (f32[2,512,256]{2,1,0:T(8,128)S(1)}, f32[2,512,256]{2,1,0:T(8,128)S(1)}, u32[]{:S(2)}, u32[]{:S(2)}) collective-permute-start(f32[2,512,256]{2,1,0:T(8,128)S(1)} %get-tuple-element.98), channel_id=1, source_target_pairs={{4,0},{8,4},{12,8},{16,12},{20,16},{24,20},{28,24},{5,1},{9,5},{13... | collective-permute-start | bytes 3145736 | tf_op jit(solution)/shard_map/ppermute | solution.py:21
  10.8 35.5 %copy-start.2 = (s32[1,1,6,2]{2,3,1,0:T(2,128)S(1)}, s32[1,1,6,2]{2,3,1,0:T(2,128)}, u32[]{:S(2)}) copy-start(s32[1,1,6,2]{2,3,1,0:T(2,128)} %param.21) | copy-start | bytes 148
  12.6 27.5 %collective-permute-start.2 = (f32[2,256,512]{2,1,0:T(8,128)S(1)}, f32[2,256,512]{2,1,0:T(8,128)S(1)}, u32[]{:S(2)}, u32[]{:S(2)}) collective-permute-start(f32[2,256,512]{2,1,0:T(8,128)S(1)} %get-tuple-element.96), channel_id=1, source_target_pairs={{1,0},{2,1},{3,2},{5,4},{6,5},{7,6},{9,8},{10,9},{11,10},{13,12},{... | collective-permute-start | bytes 3145736 | tf_op jit(solution)/shard_map/ppermute | solution.py:21
  16.0 31.8 %collective-permute-start = (f32[2,512,256]{2,1,0:T(8,128)S(1)}, f32[2,512,256]{2,1,0:T(8,128)}, u32[]{:S(2)}, u32[]{:S(2)}) collective-permute-start(f32[2,512,256]{2,1,0:T(8,128)S(1)} %get-tuple-element.99), channel_id=1, source_target_pairs={{4,0},{8,4},{12,8},{16,12},{20,16},{24,20},{28,24},{5,1},{9,5},{13... | collective-permute-start | bytes 3145736 | tf_op jit(solution)/shard_map/ppermute | solution.py:21
  27.7 1.0 copy-start
  40.1 6.2 %copy-start.1 = (f32[2,256,512]{2,1,0:T(8,128)}, f32[2,256,512]{2,1,0:T(8,128)S(1)}, u32[]{:S(2)}) copy-start(f32[2,256,512]{2,1,0:T(8,128)S(1)} %collective-permute-done.2.low) | copy-start | bytes 3145732
  40.1 38.0 %collective-permute-start.4 = (f32[2,256,768]{2,1,0:T(8,128)S(1)}, f32[2,256,768]{2,1,0:T(8,128)}, u32[]{:S(2)}, u32[]{:S(2)}) collective-permute-start(f32[2,256,768]{2,1,0:T(8,128)S(1)} %pad_maximum_fusion), channel_id=1, source_target_pairs={{1,0},{2,1},{3,2},{5,4},{6,5},{7,6},{9,8},{10,9},{11,10},{13,12},{... | collective-permute-start | bytes 4718600 | tf_op jit(solution)/shard_map/ppermute | solution.py:21
  44.4 8.6 %collective-permute-start.3 = (f32[2,256,256]{2,1,0:T(8,128)S(1)}, f32[2,256,256]{2,1,0:T(8,128)}, u32[]{:S(2)}, u32[]{:S(2)}) collective-permute-start(f32[2,256,256]{2,1,0:T(8,128)S(1)} %slice.227), channel_id=1, source_target_pairs={{4,0},{8,4},{12,8},{16,12},{20,16},{24,20},{28,24},{5,1},{9,5},{13... | collective-permute-start | bytes 1572872 | tf_op jit(solution)/shard_map/ppermute | solution.py:21
  136.2 2.0 collective-permute-start.11
  136.3 68.5 %collective-permute-start.6 = (f32[2,256,768]{2,1,0:T(8,128)}, f32[2,256,768]{2,1,0:T(8,128)S(1)}, u32[]{:S(2)}, u32[]{:S(2)}) collective-permute-start(f32[2,256,768]{2,1,0:T(8,128)} %get-tuple-element.91), channel_id=1, source_target_pairs={{0,1},{1,2},{2,3},{4,5},{5,6},{6,7},{8,9},{9,10},{10,11},{12,13},{... | collective-permute-start | bytes 4718600 | tf_op jit(solution)/shard_map/ppermute | solution.py:21
  139.5 8.8 %collective-permute-start.12 = (f32[2,2,2,32,256]{4,3,1,0,2:T(8,128)S(1)}, f32[2,2,2,32,256]{4,3,1,0,2:T(8,128)S(1)}, u32[]{:S(2)}, u32[]{:S(2)}) collective-permute-start(f32[2,2,2,32,256]{4,3,1,0,2:T(8,128)S(1)} %bitcast.45), channel_id=1, source_target_pairs={{0,8},{4,12},{8,0},{12,4},{16,24},{20,28},{24,16},{28,20},{1,9},{5... | collective-permute-start | bytes 786440 | tf_op jit(solution)/shard_map/ppermute | solution.py:269
  141.3 38.7 %collective-permute-start.5 = (f32[2,512,256]{2,1,0:T(8,128)}, f32[2,512,256]{2,1,0:T(8,128)S(1)}, u32[]{:S(2)}, u32[]{:S(2)}) collective-permute-start(f32[2,512,256]{2,1,0:T(8,128)} %get-tuple-element.90), channel_id=1, source_target_pairs={{0,4},{4,8},{8,12},{12,16},{16,20},{20,24},{24,28},{1,5},{5,9},{9,... | collective-permute-start | bytes 3145736 | tf_op jit(solution)/shard_map/ppermute | solution.py:21
  143.4 24.1 %collective-permute-start.9 = (f32[2,256,256]{2,1,0:T(8,128)}, f32[2,256,256]{2,1,0:T(8,128)}, u32[]{:S(2)}, u32[]{:S(2)}) collective-permute-start(f32[2,256,256]{2,1,0:T(8,128)} %get-tuple-element.94), channel_id=1, source_target_pairs={{0,4},{4,8},{8,12},{12,16},{16,20},{20,24},{24,28},{1,5},{5,9},{9,... | collective-permute-start | bytes 1572872 | tf_op jit(solution)/shard_map/ppermute | solution.py:21
  148.3 7.4 %collective-permute-start.13 = (f32[2,2,32,256]{3,2,1,0:T(8,128)S(1)}, f32[2,2,32,256]{3,2,1,0:T(8,128)S(1)}, u32[]{:S(2)}, u32[]{:S(2)}) collective-permute-start(f32[2,2,32,256]{3,2,1,0:T(8,128)S(1)} %dynamic-slice_bitcast_fusion.1), channel_id=1, source_target_pairs={{0,16},{4,20},{8,24},{12,28},{16,0},{20,4},{24,8},{28,12},{1,17},{... | collective-permute-start | bytes 393224 | tf_op jit(solution)/shard_map/ppermute | solution.py:269
  148.4 60.8 %collective-permute-start.7 = (f32[2,512,256]{2,1,0:T(8,128)}, f32[2,512,256]{2,1,0:T(8,128)S(1)}, u32[]{:S(2)}, u32[]{:S(2)}) collective-permute-start(f32[2,512,256]{2,1,0:T(8,128)} %get-tuple-element.92), channel_id=1, source_target_pairs={{0,4},{4,8},{8,12},{12,16},{16,20},{20,24},{24,28},{1,5},{5,9},{9,... | collective-permute-start | bytes 3145736 | tf_op jit(solution)/shard_map/ppermute | solution.py:21
  155.7 20.3 %collective-permute-start.14 = (f32[2,2,32,256]{3,2,1,0:T(8,128)S(1)}, f32[2,2,32,256]{3,2,1,0:T(8,128)S(1)}, u32[]{:S(2)}, u32[]{:S(2)}) collective-permute-start(f32[2,2,32,256]{3,2,1,0:T(8,128)S(1)} %bitcast_add_fusion.3), channel_id=1, source_target_pairs={{0,1},{1,0},{2,3},{3,2},{4,5},{5,4},{6,7},{7,6},{8,9},{9,8},{10,11... | collective-permute-start | bytes 393224 | tf_op jit(solution)/shard_map/ppermute | solution.py:278
  169.6 47.7 %collective-permute-start.10 = (f32[2,256,512]{2,1,0:T(8,128)}, f32[2,256,512]{2,1,0:T(8,128)S(1)}, u32[]{:S(2)}, u32[]{:S(2)}) collective-permute-start(f32[2,256,512]{2,1,0:T(8,128)} %add_dynamic-update-slice_fusion), channel_id=1, source_target_pairs={{0,1},{1,2},{2,3},{4,5},{5,6},{6,7},{8,9},{9,10},{10,11},{12,13},{... | collective-permute-start | bytes 3145736 | tf_op jit(solution)/shard_map/ppermute | solution.py:21
  176.0 28.1 %collective-permute-start.15 = (f32[2,2,32,256]{3,2,1,0:T(8,128)S(1)}, f32[2,2,32,256]{3,2,1,0:T(8,128)S(1)}, u32[]{:S(2)}, u32[]{:S(2)}) collective-permute-start(f32[2,2,32,256]{3,2,1,0:T(8,128)S(1)} %add.96), channel_id=1, source_target_pairs={{0,2},{1,3},{2,0},{3,1},{4,6},{5,7},{6,4},{7,5},{8,10},{9,11},{10,... | collective-permute-start | bytes 393224 | tf_op jit(solution)/shard_map/ppermute | solution.py:278
  204.9 10.5 %collective-permute-start.8 = (f32[2,256,256]{2,1,0:T(8,128)S(1)}, f32[2,256,256]{2,1,0:T(8,128)S(1)}, u32[]{:S(2)}, u32[]{:S(2)}) collective-permute-start(f32[2,256,256]{2,1,0:T(8,128)S(1)} %slice.232), channel_id=1, source_target_pairs={{0,4},{4,8},{8,12},{12,16},{16,20},{20,24},{24,28},{1,5},{5,9},{9,... | collective-permute-start | bytes 1572872 | tf_op jit(solution)/shard_map/ppermute | solution.py:21
Sparse Core Ops, SparseCore 0:
  11.0 25.5 all-gather.1
